TPU v7x, 32 devices: a whole 2x2x4 slice. The times are simulated.
32 devices in a mesh: wide: 8 (over y, x, core), oct: 4 (over z).
Axes of the slice: x: 2, y: 2, z: 4, core: 2. Of those that a mesh axis runs over, the one named last changes fastest.
Arguments:
- positions: float32 [3, 65536], P(None, ('wide', 'oct'))
- masses: float32 [65536], P(('wide', 'oct')), may hold values from 0.5 to 2
- counts: int32 [256], P(('wide', 'oct')), may hold values from 64 to 256, as said below
- near_list: int32 [256, 8], P(('wide', 'oct')), may hold values from 0 to 47, as said below
- far_list: int32 [256, 16], P(('wide', 'oct')), may hold values from 0 to 127, as said below
Outputs:
- acceleration: float32 [3, 65536], P(None, ('wide', 'oct'))
Inputs may be any that keep to these rules, and one draw needn't show every extreme that they name: counts lie between 64 and 256; both ends are reached. `near_list`: on every device the lists of its blocks together name every level 0 to 5; two entries of one block never name the same block. `far_list`: on every device the lists of its blocks together name every wide level 0 to 3.
All inputs are finite; a program needn't handle non-finite values.
Results may differ from a plain program's by a relative error of at most 0.0003.
Values sent between devices are 32-bit elements; how exact they have to be, the bound alone decides.
A program may use at most 64 MiB of HBM per device.

v0:
```python
import jax
import jax.numpy as jnp
from jax import lax
from jax.sharding import PartitionSpec as P

near_soft = 0.01
far_soft = 0.25


def swapped(shard, axis, distance):
    return lax.ppermute(shard, axis, [(i, i ^ 1 << distance) for i in range(lax.axis_size(axis))])


def near_term(targets, sources, source_mass):
    delta = sources[:, :, None, :] - targets[:, :, :, None]
    dist_sq = jnp.sum(delta * delta, axis=0) + near_soft
    inverse = lax.rsqrt(dist_sq)
    weight = source_mass[:, None, :] * (inverse * inverse * inverse)
    return jnp.sum(delta * weight[None], axis=3)


def cell_moments(block_pos, block_mass):
    total = jnp.sum(block_mass, axis=1)
    centre = jnp.sum(block_pos * block_mass[None], axis=2) / total[None]
    offset = block_pos - centre[:, :, None]
    radius_sq = jnp.sum(offset * offset, axis=0)
    trace_part = jnp.sum(block_mass * radius_sq, axis=1)

    def second(first_axis, other_axis):
        return jnp.sum(block_mass * 3.0 * offset[first_axis] * offset[other_axis], axis=1)

    return jnp.stack(
        [
            total,
            centre[0],
            centre[1],
            centre[2],
            second(0, 0) - trace_part,
            second(1, 1) - trace_part,
            second(2, 2) - trace_part,
            second(0, 1),
            second(0, 2),
            second(1, 2),
        ]
    )


def far_term(targets, chosen):
    rel = targets[:, :, None, :] - chosen[1:4, :, :, None]
    dist_sq = jnp.sum(rel * rel, axis=0) + far_soft
    inverse = lax.rsqrt(dist_sq)
    inv_sq = inverse * inverse
    inv_three = inverse * inv_sq
    inv_five = inv_three * inv_sq
    inv_seven = inv_five * inv_sq
    quad = chosen[4:10][:, :, :, None]
    qr_x = quad[0] * rel[0] + quad[3] * rel[1] + quad[4] * rel[2]
    qr_y = quad[3] * rel[0] + quad[1] * rel[1] + quad[5] * rel[2]
    qr_z = quad[4] * rel[0] + quad[5] * rel[1] + quad[2] * rel[2]
    rqr = rel[0] * qr_x + rel[1] * qr_y + rel[2] * qr_z
    radial = -chosen[0][:, :, None] * inv_three - 2.5 * rqr * inv_seven
    accel = rel * radial[None] + jnp.stack([qr_x, qr_y, qr_z]) * inv_five[None]
    return jnp.sum(accel, axis=2)


def wide_partners(payload, wide_bits):
    received = []
    for bit_number in range(wide_bits):
        received.append(swapped((payload[0], payload[1]), "wide", bit_number))
    return received


def on_device(positions, masses, counts, near_list, far_list):
    blocks = counts.shape[0]
    leaf_size = positions.shape[1] // blocks
    near_count = near_list.shape[1]
    oct_size = lax.axis_size("oct")
    oct_bits = oct_size.bit_length() - 1
    wide_bits = lax.axis_size("wide").bit_length() - 1
    valid_mask = (lax.broadcasted_iota(jnp.int32, (blocks, leaf_size), 1) < counts[:, None]).astype(
        jnp.float32
    )
    block_pos = positions.reshape(3, blocks, leaf_size)
    block_mass = masses.reshape(blocks, leaf_size) * valid_mask
    payload = (block_pos, block_mass)
    wide_sets = wide_partners(payload, wide_bits)
    oct_sets = []
    for bit_number in range(oct_bits):
        oct_sets.append(swapped((payload[0], payload[1]), "oct", bit_number))
    every_set = [payload] + oct_sets + wide_sets
    stack_pos = jnp.concatenate([member_set[0] for member_set in every_set], axis=1)
    stack_mass = jnp.concatenate([member_set[1] for member_set in every_set], axis=0)
    source_pos = jnp.take(stack_pos, near_list, axis=1)
    source_mass = jnp.take(stack_mass, near_list, axis=0)
    near_sum = jnp.zeros((3, blocks, leaf_size), jnp.float32)
    for entry in range(near_count):
        near_sum = near_sum + near_term(block_pos, source_pos[:, :, entry], source_mass[:, entry])
    cells = cell_moments(block_pos, block_mass)
    group_cells = oct_size * blocks
    own_sets = [cells]
    for bit_number in range(wide_bits):
        own_sets.append(swapped(cells, "wide", bit_number))
    cell_table = lax.all_gather(jnp.concatenate(own_sets, axis=1), "oct", axis=1, tiled=True)
    far_level = far_list // group_cells
    remain = far_list % group_cells
    columns = remain // blocks * ((wide_bits + 1) * blocks) + far_level * blocks + remain % blocks
    chosen = jnp.take(cell_table, columns, axis=1)
    far_sum = far_term(block_pos, chosen)
    grav = 1.0 / (near_count * leaf_size)
    result = (near_sum + far_sum) * grav * valid_mask[None]
    return result.reshape(3, blocks * leaf_size)


def solution(mesh):
    return jax.shard_map(
        on_device,
        mesh=mesh,
        in_specs=(
            P(None, ("wide", "oct")),
            P(("wide", "oct")),
            P(("wide", "oct")),
            P(("wide", "oct"), None),
            P(("wide", "oct"), None),
        ),
        out_specs=P(None, ("wide", "oct")),
        check_vma=False,
    )
```

profile of v0, /device:TPU:0, one launch (start us, length us, event | category | flops | bytes accessed | tf_op | source)
XLA Modules:
  0.0 70.5 jit_solution(128856669520153735)
XLA Ops:
  0.0 3.0 %collective-permute-start = (f32[3,8,256]{2,0,1:T(4,128)}, f32[3,8,256]{2,0,1:T(4,128)S(1)}, u32[]{:S(2)}, u32[]{:S(2)}) collective-permute-start(f32[3,8,256]{2,0,1:T(4,128)} %bitcast.116), channel_id=1, source_target_pairs={{0,1},{1,0},{2,3},{3,2},{4,5},{5,4},{6,7},{7,6},{8,9},{9,8},{10,11... | collective-permute-start | bytes 73736 | tf_op jit(solution)/shard_map/ppermute | solution.py:11
  3.0 2.6 %collective-permute-start.1 = (f32[3,8,256]{2,0,1:T(4,128)}, f32[3,8,256]{2,0,1:T(4,128)S(1)}, u32[]{:S(2)}, u32[]{:S(2)}) collective-permute-start(f32[3,8,256]{2,0,1:T(4,128)} %bitcast.117), channel_id=1, source_target_pairs={{0,2},{1,3},{2,0},{3,1},{4,6},{5,7},{6,4},{7,5},{8,10},{9,11},{10,... | collective-permute-start | bytes 73736 | tf_op jit(solution)/shard_map/ppermute | solution.py:11
  5.6 0.7 reshape.233
  6.3 0.7 %constant_dynamic-update-slice_fusion.11 = (f32[48,256]{1,0:T(8,128)S(1)}, f32[8,256]{1,0:T(8,128)S(1)}) fusion(f32[8,256]{1,0:T(8,128)S(1)} %reshape.233, s32[8]{0:T(128)} %param.7), kind=kLoop, calls=%fused_computation.91 | loop fusion | flops 4095 | bytes 24608
  7.0 0.9 %constant_dynamic-update-slice_fusion.5 = (f32[3,48,256]{2,0,1:T(4,128)S(1)}, f32[3,8]{0,1:T(8,128)S(1)}) fusion(f32[3,8,256]{2,0,1:T(4,128)} %bitcast.118, f32[8,256]{1,0:T(8,128)S(1)} %get-tuple-element.29), kind=kLoop, calls=%fused_computation.85 | loop fusion | flops 12263 | bytes 69632
  8.2 0.8 %broadcast_subtract_fusion.1 = f32[3,8,256]{2,0,1:T(4,128)S(1)} fusion(f32[3,8,256]{2,0,1:T(4,128)} %bitcast.119, f32[3,8]{0,1:T(8,128)S(1)} %broadcast_divide_fusion), kind=kLoop, calls=%fused_computation.95 | loop fusion | flops 6144 | bytes 49248 | tf_op jit(solution)/shard_map/sub | solution.py:25
  9.1 0.8 %multiply_reduce_fusion.1 = f32[2048]{0:T(1024)S(1)} fusion(f32[3,2048]{1,0:T(4,128)} %param.5, f32[3,2048]{1,0:T(4,128)S(1)} %bitcast.126), kind=kLoop, calls=%fused_computation.78 | loop fusion | flops 16384 | bytes 57344 | tf_op jit(solution)/shard_map/reduce_sum | solution.py:26
  10.8 1.6 %collective-permute-start.11 = (f32[10,8]{0,1:T(8,128)S(1)}, f32[10,8]{0,1:T(8,128)S(1)}, u32[]{:S(2)}, u32[]{:S(2)}) collective-permute-start(f32[10,8]{0,1:T(8,128)S(1)} %stack.29), channel_id=1, source_target_pairs={{0,8},{4,12},{8,0},{12,4},{16,24},{20,28},{24,16},{28,20},{1,9},{5... | collective-permute-start | bytes 968 | tf_op jit(solution)/shard_map/ppermute | solution.py:11
  12.4 1.5 %collective-permute-start.12 = (f32[10,8]{0,1:T(8,128)S(1)}, f32[10,8]{0,1:T(8,128)S(1)}, u32[]{:S(2)}, u32[]{:S(2)}) collective-permute-start(f32[10,8]{0,1:T(8,128)S(1)} %stack.29), channel_id=1, source_target_pairs={{0,16},{4,20},{8,24},{12,28},{16,0},{20,4},{24,8},{28,12},{1,17},{... | collective-permute-start | bytes 968 | tf_op jit(solution)/shard_map/ppermute | solution.py:11
  15.4 0.7 %compare_and_fusion = (pred[8,16]{1,0:T(8,128)(4,1)S(1)}, s32[8,16]{1,0:T(8,128)S(1)}) fusion(s32[8,16]{1,0:T(8,128)} %param.9), kind=kLoop, calls=%fused_computation.154 | loop fusion | flops 6144 | bytes 1152 | tf_op jit(solution)/shard_map/jit(_take)/and | solution.py:107
  16.2 0.7 %lt.57 = s32[8,1,256]{2,1,0:T(1,128)S(1)} broadcast(s32[8]{0:T(128)} %param.7), dimensions={0} | broadcast | bytes 8224 | tf_op jit(solution)/shard_map/lt | solution.py:80
  16.9 0.8 %copy.66 = f32[3,8,256]{2,1,0:T(8,128)S(1)} copy(f32[3,8,256]{2,0,1:T(4,128)} %bitcast.120) | data formatting | bytes 49152 | tf_op jit(solution)/shard_map/reshape | solution.py:83
  18.9 13.1 %all-gather = f32[4,32,10]{1,2,0:T(8,128)S(1)} all-gather(f32[1,32,10]{1,2,0:T(8,128)S(1)} %copy.84), channel_id=1, replica_groups=mesh['wide'=8,'oct'=4] {'oct'}, dimensions={0}, use_global_device_ids=true | all-gather | bytes 6400 | tf_op jit(solution)/shard_map/all_gather | solution.py:103
  34.1 4.0 %collective-permute-done.6 = f32[8,256]{1,0:T(8,128)S(1)} collective-permute-done((f32[8,256]{1,0:T(8,128)S(1)}, f32[8,256]{1,0:T(8,128)S(1)}, u32[]{:S(2)}, u32[]{:S(2)}) %collective-permute-start.6) | collective-permute-done | bytes 8224 | tf_op jit(solution)/shard_map/ppermute | solution.py:11
  38.1 1.2 %collective-permute-done.7 = f32[8,256]{1,0:T(8,128)S(1)} collective-permute-done((f32[8,256]{1,0:T(8,128)S(1)}, f32[8,256]{1,0:T(8,128)S(1)}, u32[]{:S(2)}, u32[]{:S(2)}) %collective-permute-start.7) | collective-permute-done | bytes 8224 | tf_op jit(solution)/shard_map/ppermute | solution.py:11
  39.3 1.5 %collective-permute-start.8 = (f32[8,256]{1,0:T(8,128)S(1)}, f32[8,256]{1,0:T(8,128)S(1)}, u32[]{:S(2)}, u32[]{:S(2)}) collective-permute-start(f32[8,256]{1,0:T(8,128)S(1)} %get-tuple-element.29), channel_id=1, source_target_pairs={{0,8},{4,12},{8,0},{12,4},{16,24},{20,28},{24,16},{28,20},{1,9},{5... | collective-permute-start | bytes 24584 | tf_op jit(solution)/shard_map/ppermute | solution.py:11
  40.8 2.2 %collective-permute-done.8 = f32[8,256]{1,0:T(8,128)S(1)} collective-permute-done((f32[8,256]{1,0:T(8,128)S(1)}, f32[8,256]{1,0:T(8,128)S(1)}, u32[]{:S(2)}, u32[]{:S(2)}) %collective-permute-start.8) | collective-permute-done | bytes 8224 | tf_op jit(solution)/shard_map/ppermute | solution.py:11
  43.4 3.1 %collective-permute-done.9 = f32[8,256]{1,0:T(8,128)S(1)} collective-permute-done((f32[8,256]{1,0:T(8,128)S(1)}, f32[8,256]{1,0:T(8,128)S(1)}, u32[]{:S(2)}, u32[]{:S(2)}) %collective-permute-start.9) | collective-permute-done | bytes 8224 | tf_op jit(solution)/shard_map/ppermute | solution.py:11
  48.0 2.4 %collective-permute-done.4 = f32[3,8,256]{2,0,1:T(4,128)S(1)} collective-permute-done((f32[3,8,256]{2,0,1:T(4,128)S(1)}, f32[3,8,256]{2,0,1:T(4,128)S(1)}, u32[]{:S(2)}, u32[]{:S(2)}) %collective-permute-start.4) | collective-permute-done | bytes 24608 | tf_op jit(solution)/shard_map/ppermute | solution.py:11
  50.5 0.7 %gather_fusion = f32[64,3,256]{2,1,0:T(4,128)S(1)} fusion(f32[3,48,256]{2,0,1:T(4,128)S(1)} %constant_dynamic-update-slice_fusion, s32[1024]{0:T(1024)S(1)} %pad_clamp_fusion.1), kind=kCustom, calls=%fused_computation | custom fusion | bytes 393472 | tf_op jit(solution)/shard_map/jit(_take)/gather | solution.py:93
  51.5 2.0 %fusion.2 = (f32[8,256,256]{2,1,0:T(8,128)S(1)}, f32[8,256,256]{2,1,0:T(8,128)S(1)}) fusion(f32[3,8,256]{2,1,0:T(8,128)S(1)} %copy.67, f32[3,8,256]{2,1,0:T(8,128)S(1)} %copy.66, f32[3,8,256]{2,1,0:T(8,128)S(1)} %copy.65), kind=kLoop, calls=%fused_computation.21 | loop fusion | flops 8388608 | bytes 4268032 | tf_op jit(solution)/shard_map/reduce_sum | solution.py:16
  53.6 0.8 %fusion.16 = (f32[8,256,256]{2,1,0:T(8,128)S(1)}, f32[8,256,256]{2,1,0:T(8,128)S(1)}) fusion(f32[8,256,256]{2,1,0:T(8,128)S(1)} %get-tuple-element.14, f32[8,256]{1,0:T(8,128)S(1)} %bitcast.130, f32[8,256,256]{2,1,0:T(8,128)S(1)} %get-tuple-element.13, f32[8,256]{1,0:T(8,128)S(1)} %bitcast.129), kind=kLoop, calls=%fused_computation.43 | loop fusion | flops 4194304 | bytes 8404992 | tf_op jit(solution)/shard_map/mul | solution.py:18
  54.4 7.1 %fusion.3 = (f32[3,8,256]{2,1,0:T(8,128)S(1)}, f32[8,256,256]{2,1,0:T(8,128)S(1)}, f32[8,256,256]{2,1,0:T(8,128)S(1)}, f32[8,256,256]{2,1,0:T(8,128)S(1)}, f32[8...) fusion(f32[8,256,256]{2,1,0:T(8,128)S(1)} %get-tuple-element.70, ...), kind=kLoop, calls=%fused_computation.22 | loop fusion | flops 34590720 | bytes 17047552 | tf_op jit(solution)/shard_map/reduce_sum | solution.py:19
  63.6 6.2 %fusion.5 = (f32[3,8,256]{2,1,0:T(8,128)S(1)}, f32[3,8,256]{2,1,0:T(8,128)S(1)}, f32[3,8,256]{2,1,0:T(8,128)S(1)}, f32[3,8,256]{2,1,0:T(8,128)S(1)}, f32[3,8,256]{2,1,0:T(8,128)S(1)}, /*index=5*/f32[3,8,256]{2,1,0:T(8,128)S(1)}) fusion(f32[8,256,256]{2,1,0:T(8,128)S(1)} %fusion.18, f32[3,8,256]{2,1,0:T(8,128)S(1)} %copy.68, f32[3,8,256]{2,1,0:T(8,128)S(1)} %copy.66, ...), kind=kLoop, calls=%fused_computation.24 | loop fusion | flops 28274688 | bytes 12902400 | tf_op jit(solution)/shard_map/reduce_sum | solution.py:19
  (91 shorter events, 10.9 us)
Async XLA Ops:
  0.0 47.9 %collective-permute-start = (f32[3,8,256]{2,0,1:T(4,128)}, f32[3,8,256]{2,0,1:T(4,128)S(1)}, u32[]{:S(2)}, u32[]{:S(2)}) collective-permute-start(f32[3,8,256]{2,0,1:T(4,128)} %bitcast.116), channel_id=1, source_target_pairs={{0,1},{1,0},{2,3},{3,2},{4,5},{5,4},{6,7},{7,6},{8,9},{9,8},{10,11... | collective-permute-start | bytes 73736 | tf_op jit(solution)/shard_map/ppermute | solution.py:11
  3.0 44.9 %collective-permute-start.1 = (f32[3,8,256]{2,0,1:T(4,128)}, f32[3,8,256]{2,0,1:T(4,128)S(1)}, u32[]{:S(2)}, u32[]{:S(2)}) collective-permute-start(f32[3,8,256]{2,0,1:T(4,128)} %bitcast.117), channel_id=1, source_target_pairs={{0,2},{1,3},{2,0},{3,1},{4,6},{5,7},{6,4},{7,5},{8,10},{9,11},{10,... | collective-permute-start | bytes 73736 | tf_op jit(solution)/shard_map/ppermute | solution.py:11
  7.0 39.5 %copy-start = (f32[3,2048]{1,0:T(4,128)S(1)}, f32[3,2048]{1,0:T(4,128)}, u32[]{:S(2)}) copy-start(f32[3,2048]{1,0:T(4,128)} %param.5) | copy-start | bytes 73732
  10.8 6.9 %collective-permute-start.10 = (f32[10,8]{0,1:T(8,128)S(1)}, f32[10,8]{0,1:T(8,128)S(1)}, u32[]{:S(2)}, u32[]{:S(2)}) collective-permute-start(f32[10,8]{0,1:T(8,128)S(1)} %stack.29), channel_id=1, source_target_pairs={{0,4},{4,0},{8,12},{12,8},{16,20},{20,16},{24,28},{28,24},{1,5},{5... | collective-permute-start | bytes 968 | tf_op jit(solution)/shard_map/ppermute | solution.py:11
  10.8 7.0 %collective-permute-start.11 = (f32[10,8]{0,1:T(8,128)S(1)}, f32[10,8]{0,1:T(8,128)S(1)}, u32[]{:S(2)}, u32[]{:S(2)}) collective-permute-start(f32[10,8]{0,1:T(8,128)S(1)} %stack.29), channel_id=1, source_target_pairs={{0,8},{4,12},{8,0},{12,4},{16,24},{20,28},{24,16},{28,20},{1,9},{5... | collective-permute-start | bytes 968 | tf_op jit(solution)/shard_map/ppermute | solution.py:11
  12.4 6.0 %collective-permute-start.12 = (f32[10,8]{0,1:T(8,128)S(1)}, f32[10,8]{0,1:T(8,128)S(1)}, u32[]{:S(2)}, u32[]{:S(2)}) collective-permute-start(f32[10,8]{0,1:T(8,128)S(1)} %stack.29), channel_id=1, source_target_pairs={{0,16},{4,20},{8,24},{12,28},{16,0},{20,4},{24,8},{28,12},{1,17},{... | collective-permute-start | bytes 968 | tf_op jit(solution)/shard_map/ppermute | solution.py:11
  17.7 30.3 %collective-permute-start.2 = (f32[3,8,256]{2,0,1:T(4,128)}, f32[3,8,256]{2,0,1:T(4,128)S(1)}, u32[]{:S(2)}, u32[]{:S(2)}) collective-permute-start(f32[3,8,256]{2,0,1:T(4,128)} %bitcast.121), channel_id=1, source_target_pairs={{0,4},{4,0},{8,12},{12,8},{16,20},{20,16},{24,28},{28,24},{1,5},{5... | collective-permute-start | bytes 73736 | tf_op jit(solution)/shard_map/ppermute | solution.py:11
  17.8 30.3 %collective-permute-start.3 = (f32[3,8,256]{2,0,1:T(4,128)}, f32[3,8,256]{2,0,1:T(4,128)S(1)}, u32[]{:S(2)}, u32[]{:S(2)}) collective-permute-start(f32[3,8,256]{2,0,1:T(4,128)} %bitcast.122), channel_id=1, source_target_pairs={{0,8},{4,12},{8,0},{12,4},{16,24},{20,28},{24,16},{28,20},{1,9},{5... | collective-permute-start | bytes 73736 | tf_op jit(solution)/shard_map/ppermute | solution.py:11
  18.4 15.1 %collective-permute-start.5 = (f32[8,256]{1,0:T(8,128)S(1)}, f32[8,256]{1,0:T(8,128)S(1)}, u32[]{:S(2)}, u32[]{:S(2)}) collective-permute-start(f32[8,256]{1,0:T(8,128)S(1)} %get-tuple-element.29), channel_id=1, source_target_pairs={{0,1},{1,0},{2,3},{3,2},{4,5},{5,4},{6,7},{7,6},{8,9},{9,8},{10,11... | collective-permute-start | bytes 24584 | tf_op jit(solution)/shard_map/ppermute | solution.py:11
  33.5 4.6 %collective-permute-start.6 = (f32[8,256]{1,0:T(8,128)S(1)}, f32[8,256]{1,0:T(8,128)S(1)}, u32[]{:S(2)}, u32[]{:S(2)}) collective-permute-start(f32[8,256]{1,0:T(8,128)S(1)} %get-tuple-element.29), channel_id=1, source_target_pairs={{0,2},{1,3},{2,0},{3,1},{4,6},{5,7},{6,4},{7,5},{8,10},{9,11},{10,... | collective-permute-start | bytes 24584 | tf_op jit(solution)/shard_map/ppermute | solution.py:11
  38.1 1.2 %collective-permute-start.7 = (f32[8,256]{1,0:T(8,128)S(1)}, f32[8,256]{1,0:T(8,128)S(1)}, u32[]{:S(2)}, u32[]{:S(2)}) collective-permute-start(f32[8,256]{1,0:T(8,128)S(1)} %get-tuple-element.29), channel_id=1, source_target_pairs={{0,4},{4,0},{8,12},{12,8},{16,20},{20,16},{24,28},{28,24},{1,5},{5... | collective-permute-start | bytes 24584 | tf_op jit(solution)/shard_map/ppermute | solution.py:11
  39.3 3.7 %collective-permute-start.8 = (f32[8,256]{1,0:T(8,128)S(1)}, f32[8,256]{1,0:T(8,128)S(1)}, u32[]{:S(2)}, u32[]{:S(2)}) collective-permute-start(f32[8,256]{1,0:T(8,128)S(1)} %get-tuple-element.29), channel_id=1, source_target_pairs={{0,8},{4,12},{8,0},{12,4},{16,24},{20,28},{24,16},{28,20},{1,9},{5... | collective-permute-start | bytes 24584 | tf_op jit(solution)/shard_map/ppermute | solution.py:11
  42.9 3.7 %collective-permute-start.9 = (f32[8,256]{1,0:T(8,128)S(1)}, f32[8,256]{1,0:T(8,128)S(1)}, u32[]{:S(2)}, u32[]{:S(2)}) collective-permute-start(f32[8,256]{1,0:T(8,128)S(1)} %get-tuple-element.29), channel_id=1, source_target_pairs={{0,16},{4,20},{8,24},{12,28},{16,0},{20,4},{24,8},{28,12},{1,17},{... | collective-permute-start | bytes 24584 | tf_op jit(solution)/shard_map/ppermute | solution.py:11
  46.6 3.9 %collective-permute-start.4 = (f32[3,8,256]{2,0,1:T(4,128)S(1)}, f32[3,8,256]{2,0,1:T(4,128)S(1)}, u32[]{:S(2)}, u32[]{:S(2)}) collective-permute-start(f32[3,8,256]{2,0,1:T(4,128)S(1)} %bitcast.123), channel_id=1, source_target_pairs={{0,16},{4,20},{8,24},{12,28},{16,0},{20,4},{24,8},{28,12},{1,17},{... | collective-permute-start | bytes 73736 | tf_op jit(solution)/shard_map/ppermute | solution.py:11
where the time goes:
time: 71.1 us; the launch traced here: 70.5 us
  other arithmetic  25.4 us (36%)
  blocking collectives  13.1 us (18%)
  starting transfers between devices  13 us (18%)
  waiting for transfers between devices  12.9 us (18%)
  local copies, waits for them, and re-layouts  5.67 us (8%)
    reduce_sum x2, other arithmetic, near_term(): return jnp.sum(delta * weight[None], axis=3)  13.3 us
    all_gather x1, blocking collectives, on_device(): lax.all_gather(jnp.concatenate(own_sets, axis=1), 'oct', axis=1, tiled=True)  13.1 us
    ppermute x13, starting transfers between devices, swapped(): lax.ppermute(shard, axis, [(i, i ^ 1 << distance) for i in range(lax.axis...  13 us
    ppermute x13, waiting for transfers between devices, swapped(): lax.ppermute(shard, axis, [(i, i ^ 1 << distance) for i in range(lax.axis...  12.9 us
    mul x7, other arithmetic, near_term(): weight = source_mass[:, None, :] * (inverse * inverse * inverse)  2.93 us
    reduce_sum x1, other arithmetic, near_term(): dist_sq = jnp.sum(delta * delta, axis=0) + near_soft  2.02 us
    unnamed x4, other arithmetic  1.67 us
  transfers between devices with their start and end apart: 13, of which 5 were waited for; matrix products, arithmetic and copies ran while one was open for 16% of the time, Pallas kernels for 0%

commit v1 on v0

v1 whole, which is shorter than its diff:
```python
import functools

import jax
import jax.numpy as jnp
from jax import lax
from jax.experimental import pallas as pl
from jax.experimental.pallas import tpu as pltpu
from jax.sharding import PartitionSpec as P

NEAR_SOFT = 0.01
FAR_SOFT = 0.25
MESH = pl.DeviceIdType.MESH
TILE = 8
LANES = 128
CELL = 10
BF = jnp.bfloat16
F32 = jnp.float32
NT = (((1,), (1,)), ((), ()))


def split3(a):
    one = a.astype(BF).astype(F32)
    rest = a - one
    two = rest.astype(BF).astype(F32)
    return one, two, rest - two


def dot(a, b):
    return jnp.dot(a, b, preferred_element_type=F32)


def partners(wide, octs):
    flips = [0] + [1 << k for k in range(wide.bit_length() - 1)]
    return [(i, f, x) for i, f in enumerate(flips) for x in range(octs) if f or x]


def kernel(
    wide, octs, cnt_ref, near_ref, far_ref, pos_ref, mass_ref, out_ref,
    src, soa, feat, centre, cells, chosen, param, send_n, recv_n, send_c, recv_c,
):
    blocks, near = near_ref.shape
    far = far_ref.shape[1]
    leaf = pos_ref.shape[1] // blocks
    w, o = lax.axis_index("wide"), lax.axis_index("oct")
    reach = partners(wide, octs)
    barrier = pltpu.get_barrier_semaphore()
    for _, f, x in reach:
        pl.semaphore_signal(barrier, inc=1, device_id=(w ^ f, o ^ x), device_id_type=MESH)

    lane = lax.broadcasted_iota(jnp.int32, (1, leaf), 1)
    for b in range(blocks):
        cols = slice(b * leaf, (b + 1) * leaf)
        row = b % 2 * 4
        xyz = pos_ref[:, cols]
        live = jnp.where(lane < cnt_ref[b], mass_ref[:, cols], 0.0)
        src[0, b // 2, row : row + 3, :] = xyz
        src[0, b // 2, row + 3 : row + 4, :] = live
        for a in range(3):
            soa[a, b : b + 1, :] = xyz[a : a + 1]
        soa[3, b : b + 1, :] = live

    mass = soa[3]
    total = jnp.sum(mass, axis=1, keepdims=True)
    mid = [jnp.sum(mass * soa[a], axis=1, keepdims=True) / total for a in range(3)]
    off = [soa[a] - mid[a] for a in range(3)]
    radius_sq = off[0] * off[0] + off[1] * off[1] + off[2] * off[2]
    trace = jnp.sum(mass * radius_sq, axis=1, keepdims=True)

    def second(i, j):
        return jnp.sum(mass * 3.0 * off[i] * off[j], axis=1, keepdims=True)

    moments = [total] + mid
    moments += [second(a, a) - trace for a in range(3)]
    moments += [second(0, 1), second(0, 2), second(1, 2)]
    at = lax.broadcasted_iota(jnp.int32, (blocks, LANES), 1)
    held = jnp.zeros((blocks, LANES), F32)
    for k, moment in enumerate(moments):
        held = jnp.where(at // blocks == k, moment, held)
    held = jnp.where(at % blocks == lax.broadcasted_iota(jnp.int32, (blocks, LANES), 0), held, 0.0)
    cells[0] = jnp.sum(held, axis=0, keepdims=True)

    pl.semaphore_wait(barrier, len(reach))
    copies = []
    flips = [(0, 1 << k) for k in range(octs.bit_length() - 1)]
    flips += [(1 << k, 0) for k in range(wide.bit_length() - 1)]
    for k, (f, x) in enumerate(flips):
        copies.append(pltpu.make_async_remote_copy(
            src_ref=src.at[0], dst_ref=src.at[k + 1], send_sem=send_n.at[k], recv_sem=recv_n.at[k],
            device_id=(w ^ f, o ^ x), device_id_type=MESH,
        ))
    for k, (i, f, x) in enumerate(reach):
        copies.append(pltpu.make_async_remote_copy(
            src_ref=cells.at[0], dst_ref=cells.at[i * octs + x], send_sem=send_c.at[k], recv_sem=recv_c.at[k],
            device_id=(w ^ f, o ^ x), device_id_type=MESH,
        ))
    for copy in copies:
        copy.start()

    sub = lax.broadcasted_iota(jnp.int32, (TILE, leaf), 0)
    for b in range(blocks):
        c = [jnp.broadcast_to(mid[a][b : b + 1], (1, leaf)) for a in range(3)]
        rows = jnp.where(sub == 0, c[0], jnp.where(sub == 1, c[1], jnp.where(sub == 2, c[2], 0.0)))
        centre[b] = rows
        p = [off[a][b : b + 1] for a in range(3)]
        norm = radius_sq[b : b + 1] + NEAR_SOFT
        t = jnp.where(sub == 0, p[0], jnp.where(sub == 1, p[1], p[2])) * -2.0
        t = jnp.where(sub < 3, t, jnp.where(sub == 3, 1.0, jnp.where(sub == 4, norm, 0.0)))
        t1, t2, t3 = split3(t)
        stack = jnp.concatenate([t1, t2, t3, t1, t2, t1], axis=0)
        feat[b] = stack.T.astype(BF)

    for copy in copies:
        copy.wait()

    slot_at = lax.broadcasted_iota(jnp.int32, (1, LANES), 1) % blocks

    def choose(b, carry):
        for v in range(far):
            name = far_ref[b, v]
            rest = name % (octs * blocks)
            which = name // (octs * blocks) * octs + ((rest // blocks) ^ o)
            chosen[b, v : v + 1, :] = jnp.where(slot_at == rest % blocks, cells[which], 0.0)
        return carry

    lax.fori_loop(0, blocks, choose, 0)
    spread = (
        lax.broadcasted_iota(jnp.int32, (LANES, LANES), 0) // blocks
        == lax.broadcasted_iota(jnp.int32, (LANES, LANES), 1)
    ).astype(F32).astype(BF)
    picked = [part.astype(BF) for part in split3(chosen[...].reshape(blocks * far, LANES))]
    param[...] = (dot(picked[0], spread) + dot(picked[1], spread) + dot(picked[2], spread)).reshape(
        blocks, far, LANES
    )

    scale = 1.0 / (near * leaf)

    def target(b, carry):
        mid_b = centre[b]
        grid = feat[b]
        acc = jnp.zeros((4 * TILE, leaf), F32)
        for v in range(near):
            name = near_ref[b, v]
            slot = name % blocks
            raw = src[name // blocks, slot // 2]
            raw = jnp.where(slot % 2 == 1, pltpu.roll(raw, 4, 0), raw)
            m = raw[3:4]
            q = jnp.where(sub < 3, raw - mid_b, 0.0)
            norm = jnp.sum(q * q, axis=0, keepdims=True)
            s = jnp.where(sub < 3, q, jnp.where(sub == 3, norm, jnp.where(sub == 4, 1.0, 0.0)))
            s1, s2, s3 = split3(s)
            stack = jnp.concatenate([s1, s1, s1, s2, s2, s3], axis=0).astype(BF)
            a1, a2, a3 = split3(jnp.where(sub < 3, q, jnp.where(sub == 3, 1.0, 0.0)) * m)
            amount = jnp.concatenate([a1, a2, a3, jnp.zeros_like(a1)], axis=0).astype(BF)
            dist_sq = jnp.maximum(dot(grid, stack), NEAR_SOFT)
            inverse = lax.rsqrt(dist_sq)
            weight = inverse * inverse * inverse
            high = weight.astype(BF)
            low = (weight - high.astype(F32)).astype(BF)
            acc += lax.dot_general(amount, high, NT, preferred_element_type=F32)
            acc += lax.dot_general(amount, low, NT, preferred_element_type=F32)
        acc = acc[:TILE] + acc[TILE : 2 * TILE] + acc[2 * TILE : 3 * TILE]
        pair = src[0, b // 2]
        own = jnp.where(b % 2 == 1, pltpu.roll(pair, 4, 0), pair)
        near_sum = acc[:3] - (own - mid_b)[:3] * acc[3:4]

        par = param[b]
        col = [par[:, k : k + 1] for k in range(CELL)]
        rel = [own[a : a + 1] - col[1 + a] for a in range(3)]
        dist_sq = rel[0] * rel[0] + rel[1] * rel[1] + rel[2] * rel[2] + FAR_SOFT
        inverse = lax.rsqrt(dist_sq)
        inv_sq = inverse * inverse
        inv_three = inverse * inv_sq
        inv_five = inv_three * inv_sq
        inv_seven = inv_five * inv_sq
        xx, yy, zz, xy, xz, yz = col[4:]
        qr = [
            xx * rel[0] + xy * rel[1] + xz * rel[2],
            xy * rel[0] + yy * rel[1] + yz * rel[2],
            xz * rel[0] + yz * rel[1] + zz * rel[2],
        ]
        rqr = rel[0] * qr[0] + rel[1] * qr[1] + rel[2] * qr[2]
        radial = -col[0] * inv_three - 2.5 * rqr * inv_seven
        live = lane < cnt_ref[b]
        for a in range(3):
            far_sum = jnp.sum(rel[a] * radial + qr[a] * inv_five, axis=0, keepdims=True)
            result = jnp.where(live, (near_sum[a : a + 1] + far_sum) * scale, 0.0)
            out_ref[a : a + 1, pl.ds(pl.multiple_of(b * leaf, leaf), leaf)] = result
        return carry

    lax.fori_loop(0, blocks, target, 0)


def solution(mesh):
    wide, octs = mesh.shape["wide"], mesh.shape["oct"]

    def on_device(positions, masses, counts, near_list, far_list):
        blocks, near = near_list.shape
        far = far_list.shape[1]
        bodies = positions.shape[1]
        leaf = bodies // blocks
        steps = octs.bit_length() + wide.bit_length() - 2
        reach = len(partners(wide, octs))
        return pl.pallas_call(
            functools.partial(kernel, wide, octs),
            out_shape=jax.ShapeDtypeStruct((3, bodies), F32),
            in_specs=[pl.BlockSpec(memory_space=pltpu.SMEM)] * 3
            + [pl.BlockSpec(memory_space=pltpu.VMEM)] * 2,
            out_specs=pl.BlockSpec(memory_space=pltpu.VMEM),
            scratch_shapes=[
                pltpu.VMEM((steps + 1, blocks // 2, TILE, leaf), F32),
                pltpu.VMEM((4, blocks, leaf), F32),
                pltpu.VMEM((blocks, leaf, 6 * TILE), BF),
                pltpu.VMEM((blocks, TILE, leaf), F32),
                pltpu.VMEM((reach + 1, 1, LANES), F32),
                pltpu.VMEM((blocks, far, LANES), F32),
                pltpu.VMEM((blocks, far, LANES), F32),
                pltpu.SemaphoreType.DMA((steps,)),
                pltpu.SemaphoreType.DMA((steps,)),
                pltpu.SemaphoreType.DMA((reach,)),
                pltpu.SemaphoreType.DMA((reach,)),
            ],
            compiler_params=pltpu.CompilerParams(
                collective_id=0, has_side_effects=True, vmem_limit_bytes=32 * 1024 * 1024
            ),
        )(counts, near_list, far_list, positions, masses.reshape(1, bodies))

    return jax.shard_map(
        on_device,
        mesh=mesh,
        in_specs=(
            P(None, ("wide", "oct")),
            P(("wide", "oct")),
            P(("wide", "oct")),
            P(("wide", "oct"), None),
            P(("wide", "oct"), None),
        ),
        out_specs=P(None, ("wide", "oct")),
        check_vma=False,
    )
```

time: 71.1 us -> 30.6 us (0.43)
  Pallas kernels: 0 us -> 26.2 us
  other arithmetic: 25.4 us -> 0 us
  blocking collectives: 13.1 us -> 0 us
  starting transfers between devices: 13 us -> 0 us
  waiting for transfers between devices: 12.9 us -> 0 us
  local copies, waits for them, and re-layouts: 5.67 us -> 4.1 us
    pallas_call x0 -> x1, Pallas kernels: none -> 26.2 us  [on_device(): pl.pallas_call(functools.partial(kernel, wide, octs), out_shape=jax.Shape...]
    reduce_sum x7 -> x0, other arithmetic: 16.6 us -> none  [the longest x2 13.3 us: near_term(): return jnp.sum(delta * weight[None], axis=3)]
    all_gather x1 -> x0, blocking collectives: 13.1 us -> none  [on_device(): lax.all_gather(jnp.concatenate(own_sets, axis=1), 'oct', axis=1, tiled=True)]
    ppermute x13 -> x0, starting transfers between devices: 13 us -> none  [swapped(): lax.ppermute(shard, axis, [(i, i ^ 1 << distance) for i in range(lax.axis...]
    ppermute x13 -> x0, waiting for transfers between devices: 12.9 us -> none  [swapped(): lax.ppermute(shard, axis, [(i, i ^ 1 << distance) for i in range(lax.axis...]
    unnamed x19 -> x11, local copies, waits for them, and re-layouts: 0.19 us -> 4.1 us
    mul x12 -> x0, other arithmetic: 3.79 us -> none  [the longest x7 2.93 us: near_term(): weight = source_mass[:, None, :] * (inverse * inverse * inverse)]
    gather x4 -> x0, local copies, waits for them, and re-layouts: 2.12 us -> none  [the longest x2 0.76 us: on_device(): chosen = jnp.take(cell_table, columns, axis=1)]
  transfers between devices with their start and end apart: 13 -> 0, of which waited for: 5 -> 0; matrix products, arithmetic and copies ran while one was open for 16% -> 0% of each run, Pallas kernels for 0% -> 0%
where the time goes in v1:
time: 30.6 us; the launch traced here: 30.3 us
  Pallas kernels  26.2 us (86%)
  local copies, waits for them, and re-layouts  4.1 us (13%)
    pallas_call x1, Pallas kernels, on_device(): pl.pallas_call(functools.partial(kernel, wide, octs), out_shape=jax.Shape...  26.2 us
    unnamed x11, local copies, waits for them, and re-layouts  4.1 us

profile of v1, /device:TPU:0, one launch (start us, length us, event | category | flops | bytes accessed | tf_op | source)
XLA Modules:
  0.0 30.3 jit_solution(5671639208695078614)
XLA Ops:
  0.0 0.0 copy-start.4
  0.0 0.7 %copy-done.4 = s32[8]{0:T(128)S(1)} copy-done((s32[8]{0:T(128)S(1)}, s32[8]{0:T(128)}, u32[]{:S(2)}) %copy-start.4) | copy-done | bytes 56
  0.7 0.0 copy-start
  0.7 0.8 %copy-done = f32[3,2048]{1,0:T(4,128)S(1)} copy-done((f32[3,2048]{1,0:T(4,128)S(1)}, f32[3,2048]{1,0:T(4,128)}, u32[]{:S(2)}) %copy-start) | copy-done | bytes 24600
  1.4 0.0 copy-start.1
  1.4 0.7 %copy-done.1 = f32[2048]{0:T(1024)S(1)} copy-done((f32[2048]{0:T(1024)S(1)}, f32[2048]{0:T(1024)}, u32[]{:S(2)}) %copy-start.1) | copy-done | bytes 8216
  2.1 0.0 copy-start.2
  2.1 0.7 %copy-done.2 = s32[8,8]{1,0:T(8,128)S(1)} copy-done((s32[8,8]{1,0:T(8,128)S(1)}, s32[8,8]{1,0:T(8,128)}, u32[]{:S(2)}) %copy-start.2) | copy-done | bytes 280
  2.8 0.0 copy-start.3
  2.8 0.7 %copy-done.3 = s32[8,16]{1,0:T(8,128)S(1)} copy-done((s32[8,16]{1,0:T(8,128)S(1)}, s32[8,16]{1,0:T(8,128)}, u32[]{:S(2)}) %copy-start.3) | copy-done | bytes 536
  3.5 26.2 %shard_map.55 = f32[3,2048]{1,0:T(4,128)S(1)} custom-call(s32[8]{0:T(128)S(1)} %copy-done.4, s32[8,8]{1,0:T(8,128)S(1)} %copy-done.2, s32[8,16]{1,0:T(8,128)S(1)} %copy-done.3, f32[3,2048]{1,0:T(4,128)S(1)} %copy-done, f32[1,2048]{1,0:T(1,128)S(1)} %bitcast.1), custom_call_target="tpu_custom_call" | custom-call | tf_op jit(solution)/shard_map/pallas_call | solution.py:203
  29.7 0.6 %copy.7 = f32[3,2048]{1,0:T(4,128)} copy(f32[3,2048]{1,0:T(4,128)S(1)} %shard_map.55) | data formatting | bytes 49152
Async XLA Ops:
  0.0 0.7 %copy-start.4 = (s32[8]{0:T(128)S(1)}, s32[8]{0:T(128)}, u32[]{:S(2)}) copy-start(s32[8]{0:T(128)} %cnt_ref.1) | copy-start | bytes 100
  0.7 0.8 %copy-start = (f32[3,2048]{1,0:T(4,128)S(1)}, f32[3,2048]{1,0:T(4,128)}, u32[]{:S(2)}) copy-start(f32[3,2048]{1,0:T(4,128)} %pos_ref.1) | copy-start | bytes 73732
  1.4 0.7 %copy-start.1 = (f32[2048]{0:T(1024)S(1)}, f32[2048]{0:T(1024)}, u32[]{:S(2)}) copy-start(f32[2048]{0:T(1024)} %param.6) | copy-start | bytes 24580
  2.1 0.7 %copy-start.2 = (s32[8,8]{1,0:T(8,128)S(1)}, s32[8,8]{1,0:T(8,128)}, u32[]{:S(2)}) copy-start(s32[8,8]{1,0:T(8,128)} %near_ref.1) | copy-start | bytes 772
  2.8 0.7 %copy-start.3 = (s32[8,16]{1,0:T(8,128)S(1)}, s32[8,16]{1,0:T(8,128)}, u32[]{:S(2)}) copy-start(s32[8,16]{1,0:T(8,128)} %far_ref.1) | copy-start | bytes 1540

commit v2 on v1

v2 whole, which is shorter than its diff:
```python
import functools

import jax
import jax.numpy as jnp
from jax import lax
from jax.experimental import pallas as pl
from jax.experimental.pallas import tpu as pltpu
from jax.sharding import PartitionSpec as P

NEAR_SOFT = 0.01
FAR_SOFT = 0.25
MESH = pl.DeviceIdType.MESH
TILE = 8
LANES = 128
CELL = 10
BF = jnp.bfloat16
F32 = jnp.float32
NT = (((1,), (1,)), ((), ()))


def split3(a):
    one = a.astype(BF).astype(F32)
    rest = a - one
    two = rest.astype(BF).astype(F32)
    return one, two, rest - two


def dot(a, b):
    return jnp.dot(a, b, preferred_element_type=F32)


def kernel(
    wide, octs, cnt_in, near_in, far_in, pos_in, mass_in, out_ref,
    cnt_ref, near_ref, far_ref, pos_ref, mass_ref,
    src, soa, feat, centre, cells, picks, slots, fields, load, send_n, recv_n, send_c, recv_c, send_r, recv_r,
):
    blocks, near = near_ref.shape
    far = far_ref.shape[1]
    leaf = pos_ref.shape[1] // blocks
    w, o = lax.axis_index("wide"), lax.axis_index("oct")
    flips = [(0, 1 << k) for k in range(octs.bit_length() - 1)]
    flips += [(1 << k, 0) for k in range(wide.bit_length() - 1)]
    sets = wide.bit_length()
    barrier = pltpu.get_barrier_semaphore()
    for f, x in flips:
        pl.semaphore_signal(barrier, inc=1, device_id=(w ^ f, o ^ x), device_id_type=MESH)

    taken = [
        pltpu.make_async_copy(a, b, load.at[k])
        for k, (a, b) in enumerate([
            (pos_in, pos_ref), (mass_in, mass_ref), (cnt_in, cnt_ref), (near_in, near_ref), (far_in, far_ref),
        ])
    ]
    for copy in taken:
        copy.start()
    for copy in taken[:3]:
        copy.wait()

    lane = lax.broadcasted_iota(jnp.int32, (1, leaf), 1)
    for b in range(blocks):
        cols = slice(b * leaf, (b + 1) * leaf)
        row = b % 2 * 4
        xyz = pos_ref[:, cols]
        live = jnp.where(lane < cnt_ref[b], mass_ref[:, cols], 0.0)
        src[0, b // 2, row : row + 3, :] = xyz
        src[0, b // 2, row + 3 : row + 4, :] = live
        for a in range(3):
            soa[a, b : b + 1, :] = xyz[a : a + 1]
        soa[3, b : b + 1, :] = live

    pl.semaphore_wait(barrier, len(flips))
    copies = []
    for k, (f, x) in enumerate(flips):
        copies.append(pltpu.make_async_remote_copy(
            src_ref=src.at[0], dst_ref=src.at[k + 1], send_sem=send_n.at[k], recv_sem=recv_n.at[k],
            device_id=(w ^ f, o ^ x), device_id_type=MESH,
        ))
    for copy in copies:
        copy.start()

    mass = soa[3]
    total = jnp.sum(mass, axis=1, keepdims=True)
    mid = [jnp.sum(mass * soa[a], axis=1, keepdims=True) / total for a in range(3)]
    off = [soa[a] - mid[a] for a in range(3)]
    radius_sq = off[0] * off[0] + off[1] * off[1] + off[2] * off[2]
    trace = jnp.sum(mass * radius_sq, axis=1, keepdims=True)

    def second(i, j):
        return jnp.sum(mass * 3.0 * off[i] * off[j], axis=1, keepdims=True)

    moments = [total] + mid
    moments += [second(a, a) - trace for a in range(3)]
    moments += [second(0, 1), second(0, 2), second(1, 2)]
    at = lax.broadcasted_iota(jnp.int32, (blocks, LANES), 1)
    held = jnp.zeros((blocks, LANES), F32)
    for k, moment in enumerate(moments):
        held = jnp.where(at // blocks == k, moment, held)
    held = jnp.where(at % blocks == lax.broadcasted_iota(jnp.int32, (blocks, LANES), 0), held, 0.0)
    cells[0] = jnp.sum(held, axis=0, keepdims=True)

    for k in range(sets - 1):
        copies.append(pltpu.make_async_remote_copy(
            src_ref=cells.at[0], dst_ref=cells.at[k + 1], send_sem=send_c.at[k], recv_sem=recv_c.at[k],
            device_id=(w ^ 1 << k, o), device_id_type=MESH,
        ))
    for copy in copies[len(flips) :]:
        copy.start()

    for copy in taken[3:]:
        copy.wait()
    lane_at = lax.broadcasted_iota(jnp.int32, (1, LANES), 1)
    set_at = lax.broadcasted_iota(jnp.int32, (1, sets * octs), 1)

    def name_cells(b, carry):
        for v in range(far):
            name = far_ref[b, v]
            rest = name % (octs * blocks)
            which = ((rest // blocks) ^ o) * sets + name // (octs * blocks)
            picks[b, v : v + 1, :] = jnp.where(set_at == which, 1.0, 0.0)
            slots[b, v : v + 1, :] = jnp.where(lane_at % blocks == rest % blocks, 1.0, 0.0)
        return carry

    lax.fori_loop(0, blocks, name_cells, 0)

    sub = lax.broadcasted_iota(jnp.int32, (TILE, leaf), 0)
    for b in range(blocks):
        c = [jnp.broadcast_to(mid[a][b : b + 1], (1, leaf)) for a in range(3)]
        rows = jnp.where(sub == 0, c[0], jnp.where(sub == 1, c[1], jnp.where(sub == 2, c[2], 0.0)))
        centre[b] = rows
        p = [off[a][b : b + 1] for a in range(3)]
        norm = radius_sq[b : b + 1] + NEAR_SOFT
        t = jnp.where(sub == 0, p[0], jnp.where(sub == 1, p[1], p[2])) * -2.0
        t = jnp.where(sub < 3, t, jnp.where(sub == 3, 1.0, jnp.where(sub == 4, norm, 0.0)))
        t1, t2, t3 = split3(t)
        stack = jnp.concatenate([t1, t2, t3, t1, t2, t1], axis=0)
        feat[b] = stack.astype(BF)

    for copy in copies:
        copy.wait()

    def near_field(b, carry):
        mid_b = centre[b]
        grid = feat[b]
        acc = jnp.zeros((4 * TILE, leaf), F32)
        for v in range(near):
            name = near_ref[b, v]
            slot = name % blocks
            raw = src[name // blocks, slot // 2]
            raw = jnp.where(slot % 2 == 1, pltpu.roll(raw, 4, 0), raw)
            m = raw[3:4]
            q = jnp.where(sub < 3, raw - mid_b, 0.0)
            norm = jnp.sum(q * q, axis=0, keepdims=True)
            s = jnp.where(sub < 3, q, jnp.where(sub == 3, norm, jnp.where(sub == 4, 1.0, 0.0)))
            s1, s2, s3 = split3(s)
            stack = jnp.concatenate([s1, s1, s1, s2, s2, s3], axis=0).astype(BF)
            a1, a2, a3 = split3(jnp.where(sub < 3, q, jnp.where(sub == 3, 1.0, 0.0)) * m)
            amount = jnp.concatenate([a1, a2, a3, jnp.zeros_like(a1)], axis=0).astype(BF)
            dist_sq = jnp.maximum(lax.dot_general(stack, grid, (((0,),(0,)),((),())), preferred_element_type=F32), NEAR_SOFT)
            inverse = lax.rsqrt(dist_sq)
            weight = inverse * inverse * inverse
            high = weight.astype(BF)
            low = (weight - high.astype(F32)).astype(BF)
            acc += dot(amount, high)
            acc += dot(amount, low)
        acc = acc[:TILE] + acc[TILE : 2 * TILE] + acc[2 * TILE : 3 * TILE]
        pair = src[0, b // 2]
        own = jnp.where(b % 2 == 1, pltpu.roll(pair, 4, 0), pair)
        fields[b, :3, :] = acc[:3] - (own - mid_b)[:3] * acc[3:4]
        return carry

    steps = octs.bit_length() - 1
    for k in range(steps):
        count = sets << k
        relay = pltpu.make_async_remote_copy(
            src_ref=cells.at[pl.ds(0, count)], dst_ref=cells.at[pl.ds(count, count)],
            send_sem=send_r.at[k], recv_sem=recv_r.at[k],
            device_id=(w, o ^ 1 << k), device_id_type=MESH,
        )
        relay.start()
        lax.fori_loop(k * blocks // steps, (k + 1) * blocks // steps, near_field, 0)
        relay.wait()

    table = jnp.concatenate([cells[k] for k in range(sets * octs)], axis=0)
    picked = picks[...].reshape(blocks * far, sets * octs).astype(BF)
    chosen = sum(dot(picked, part.astype(BF)) for part in split3(table))
    chosen = chosen * slots[...].reshape(blocks * far, LANES)
    spread = (
        lax.broadcasted_iota(jnp.int32, (LANES, LANES), 0) // blocks
        == lax.broadcasted_iota(jnp.int32, (LANES, LANES), 1)
    ).astype(F32).astype(BF)
    param = sum(dot(part.astype(BF), spread) for part in split3(chosen))

    scale = 1.0 / (near * leaf)
    for b in range(blocks):
        par = param[b * far : (b + 1) * far]
        own = [soa[a, b : b + 1, :] for a in range(3)]
        col = [par[:, k : k + 1] for k in range(CELL)]
        rel = [own[a] - col[1 + a] for a in range(3)]
        dist_sq = rel[0] * rel[0] + rel[1] * rel[1] + rel[2] * rel[2] + FAR_SOFT
        inverse = lax.rsqrt(dist_sq)
        inv_sq = inverse * inverse
        inv_three = inverse * inv_sq
        inv_five = inv_three * inv_sq
        inv_seven = inv_five * inv_sq
        xx, yy, zz, xy, xz, yz = col[4:]
        qr = [
            xx * rel[0] + xy * rel[1] + xz * rel[2],
            xy * rel[0] + yy * rel[1] + yz * rel[2],
            xz * rel[0] + yz * rel[1] + zz * rel[2],
        ]
        rqr = rel[0] * qr[0] + rel[1] * qr[1] + rel[2] * qr[2]
        radial = -col[0] * inv_three - 2.5 * rqr * inv_seven
        live = lane < cnt_ref[b]
        for a in range(3):
            far_sum = jnp.sum(rel[a] * radial + qr[a] * inv_five, axis=0, keepdims=True)
            result = jnp.where(live, (fields[b, a : a + 1, :] + far_sum) * scale, 0.0)
            out_ref[a : a + 1, b * leaf : (b + 1) * leaf] = result


def solution(mesh):
    wide, octs = mesh.shape["wide"], mesh.shape["oct"]

    def on_device(positions, masses, counts, near_list, far_list):
        blocks, near = near_list.shape
        far = far_list.shape[1]
        bodies = positions.shape[1]
        leaf = bodies // blocks
        steps = octs.bit_length() + wide.bit_length() - 2
        sets = wide.bit_length()
        return pl.pallas_call(
            functools.partial(kernel, wide, octs),
            out_shape=jax.ShapeDtypeStruct((3, bodies), F32),
            in_specs=[pl.BlockSpec(memory_space=pltpu.HBM)] * 5,
            out_specs=pl.BlockSpec(memory_space=pltpu.VMEM),
            scratch_shapes=[
                pltpu.SMEM((blocks,), jnp.int32),
                pltpu.SMEM((blocks, near), jnp.int32),
                pltpu.SMEM((blocks, far), jnp.int32),
                pltpu.VMEM((3, bodies), F32),
                pltpu.VMEM((1, bodies), F32),
                pltpu.VMEM((steps + 1, blocks // 2, TILE, leaf), F32),
                pltpu.VMEM((4, blocks, leaf), F32),
                pltpu.VMEM((blocks, 6 * TILE, leaf), BF),
                pltpu.VMEM((blocks, TILE, leaf), F32),
                pltpu.VMEM((sets * octs, 1, LANES), F32),
                pltpu.VMEM((blocks, far, sets * octs), F32),
                pltpu.VMEM((blocks, far, LANES), F32),
                pltpu.VMEM((blocks, TILE, leaf), F32),
                pltpu.SemaphoreType.DMA((5,)),
                pltpu.SemaphoreType.DMA((steps,)),
                pltpu.SemaphoreType.DMA((steps,)),
                pltpu.SemaphoreType.DMA((sets - 1,)),
                pltpu.SemaphoreType.DMA((sets - 1,)),
                pltpu.SemaphoreType.DMA((octs.bit_length() - 1,)),
                pltpu.SemaphoreType.DMA((octs.bit_length() - 1,)),
            ],
            compiler_params=pltpu.CompilerParams(
                collective_id=0, has_side_effects=True, vmem_limit_bytes=32 * 1024 * 1024
            ),
        )(counts, near_list, far_list, positions, masses.reshape(1, bodies))

    return jax.shard_map(
        on_device,
        mesh=mesh,
        in_specs=(
            P(None, ("wide", "oct")),
            P(("wide", "oct")),
            P(("wide", "oct")),
            P(("wide", "oct"), None),
            P(("wide", "oct"), None),
        ),
        out_specs=P(None, ("wide", "oct")),
        check_vma=False,
    )
```

time: 30.6 us -> 20.6 us (0.67)
  Pallas kernels: 26.2 us -> 16.2 us
    pallas_call x1, Pallas kernels: 26.2 us -> 16.2 us  [on_device(): pl.pallas_call(functools.partial(kernel, wide, octs), out_shape=jax.Shape...]
where the time goes in v2:
time: 20.6 us; the launch traced here: 20.3 us
  Pallas kernels  16.2 us (79%)
  local copies, waits for them, and re-layouts  4.1 us (20%)
    pallas_call x1, Pallas kernels, on_device(): pl.pallas_call(functools.partial(kernel, wide, octs), out_shape=jax.Shape...  16.2 us
    unnamed x11, local copies, waits for them, and re-layouts  4.1 us

profile of v2, /device:TPU:0, one launch (start us, length us, event | category | flops | bytes accessed | tf_op | source)
XLA Modules:
  0.0 20.3 jit_solution(11443343591875451209)
XLA Ops:
  0.0 0.0 copy-start.4
  0.0 0.7 %copy-done.4 = s32[8]{0:T(128)S(1)} copy-done((s32[8]{0:T(128)S(1)}, s32[8]{0:T(128)}, u32[]{:S(2)}) %copy-start.4) | copy-done | bytes 56
  0.7 0.0 copy-start
  0.7 0.8 %copy-done = f32[3,2048]{1,0:T(4,128)S(1)} copy-done((f32[3,2048]{1,0:T(4,128)S(1)}, f32[3,2048]{1,0:T(4,128)}, u32[]{:S(2)}) %copy-start) | copy-done | bytes 24600
  1.4 0.0 copy-start.1
  1.4 0.7 %copy-done.1 = f32[2048]{0:T(1024)S(1)} copy-done((f32[2048]{0:T(1024)S(1)}, f32[2048]{0:T(1024)}, u32[]{:S(2)}) %copy-start.1) | copy-done | bytes 8216
  2.1 0.0 copy-start.2
  2.1 0.7 %copy-done.2 = s32[8,8]{1,0:T(8,128)S(1)} copy-done((s32[8,8]{1,0:T(8,128)S(1)}, s32[8,8]{1,0:T(8,128)}, u32[]{:S(2)}) %copy-start.2) | copy-done | bytes 280
  2.8 0.0 copy-start.3
  2.8 0.7 %copy-done.3 = s32[8,16]{1,0:T(8,128)S(1)} copy-done((s32[8,16]{1,0:T(8,128)S(1)}, s32[8,16]{1,0:T(8,128)}, u32[]{:S(2)}) %copy-start.3) | copy-done | bytes 536
  3.5 16.2 %shard_map.55 = f32[3,2048]{1,0:T(4,128)S(1)} custom-call(s32[8]{0:T(128)S(1)} %copy-done.4, s32[8,8]{1,0:T(8,128)S(1)} %copy-done.2, s32[8,16]{1,0:T(8,128)S(1)} %copy-done.3, f32[3,2048]{1,0:T(4,128)S(1)} %copy-done, f32[1,2048]{1,0:T(1,128)S(1)} %bitcast.1), custom_call_target="tpu_custom_call" | custom-call | tf_op jit(solution)/shard_map/pallas_call | solution.py:230
  19.7 0.6 %copy.7 = f32[3,2048]{1,0:T(4,128)} copy(f32[3,2048]{1,0:T(4,128)S(1)} %shard_map.55) | data formatting | bytes 49152
Async XLA Ops:
  0.0 0.7 %copy-start.4 = (s32[8]{0:T(128)S(1)}, s32[8]{0:T(128)}, u32[]{:S(2)}) copy-start(s32[8]{0:T(128)} %cnt_in.1) | copy-start | bytes 100
  0.7 0.8 %copy-start = (f32[3,2048]{1,0:T(4,128)S(1)}, f32[3,2048]{1,0:T(4,128)}, u32[]{:S(2)}) copy-start(f32[3,2048]{1,0:T(4,128)} %pos_in.1) | copy-start | bytes 73732
  1.4 0.7 %copy-start.1 = (f32[2048]{0:T(1024)S(1)}, f32[2048]{0:T(1024)}, u32[]{:S(2)}) copy-start(f32[2048]{0:T(1024)} %param.6) | copy-start | bytes 24580
  2.1 0.7 %copy-start.2 = (s32[8,8]{1,0:T(8,128)S(1)}, s32[8,8]{1,0:T(8,128)}, u32[]{:S(2)}) copy-start(s32[8,8]{1,0:T(8,128)} %near_in.1) | copy-start | bytes 772
  2.8 0.7 %copy-start.3 = (s32[8,16]{1,0:T(8,128)S(1)}, s32[8,16]{1,0:T(8,128)}, u32[]{:S(2)}) copy-start(s32[8,16]{1,0:T(8,128)} %far_in.1) | copy-start | bytes 1540

commit v3 on v2

--- a/solution.py
+++ b/solution.py
@@ -42,7 +42,8 @@
     flips += [(1 << k, 0) for k in range(wide.bit_length() - 1)]
     sets = wide.bit_length()
     barrier = pltpu.get_barrier_semaphore()
-    for f, x in flips:
+    greet = flips + [(0, x) for x in range(1, octs) if x & (x - 1)]
+    for f, x in greet:
         pl.semaphore_signal(barrier, inc=1, device_id=(w ^ f, o ^ x), device_id_type=MESH)
 
     taken = [
@@ -68,7 +69,7 @@
             soa[a, b : b + 1, :] = xyz[a : a + 1]
         soa[3, b : b + 1, :] = live
 
-    pl.semaphore_wait(barrier, len(flips))
+    pl.semaphore_wait(barrier, len(greet))
     copies = []
     for k, (f, x) in enumerate(flips):
         copies.append(pltpu.make_async_remote_copy(
@@ -168,16 +169,17 @@
         fields[b, :3, :] = acc[:3] - (own - mid_b)[:3] * acc[3:4]
         return carry
 
-    steps = octs.bit_length() - 1
-    for k in range(steps):
-        count = sets << k
-        relay = pltpu.make_async_remote_copy(
-            src_ref=cells.at[pl.ds(0, count)], dst_ref=cells.at[pl.ds(count, count)],
-            send_sem=send_r.at[k], recv_sem=recv_r.at[k],
-            device_id=(w, o ^ 1 << k), device_id_type=MESH,
-        )
+    relays = []
+    for x in range(1, octs):
+        relays.append(pltpu.make_async_remote_copy(
+            src_ref=cells.at[pl.ds(0, sets)], dst_ref=cells.at[pl.ds(x * sets, sets)],
+            send_sem=send_r.at[x - 1], recv_sem=recv_r.at[x - 1],
+            device_id=(w, o ^ x), device_id_type=MESH,
+        ))
+    for relay in relays:
         relay.start()
-        lax.fori_loop(k * blocks // steps, (k + 1) * blocks // steps, near_field, 0)
+    lax.fori_loop(0, blocks, near_field, 0)
+    for relay in relays:
         relay.wait()
 
     table = jnp.concatenate([cells[k] for k in range(sets * octs)], axis=0)
@@ -251,8 +253,8 @@
                 pltpu.SemaphoreType.DMA((steps,)),
                 pltpu.SemaphoreType.DMA((sets - 1,)),
                 pltpu.SemaphoreType.DMA((sets - 1,)),
-                pltpu.SemaphoreType.DMA((octs.bit_length() - 1,)),
-                pltpu.SemaphoreType.DMA((octs.bit_length() - 1,)),
+                pltpu.SemaphoreType.DMA((octs - 1,)),
+                pltpu.SemaphoreType.DMA((octs - 1,)),
             ],
             compiler_params=pltpu.CompilerParams(
                 collective_id=0, has_side_effects=True, vmem_limit_bytes=32 * 1024 * 1024

time: 20.6 us -> 21.2 us (1.029)
  Pallas kernels: 16.2 us -> 16.8 us
    pallas_call x1, Pallas kernels: 16.2 us -> 16.8 us  [on_device(): pl.pallas_call(functools.partial(kernel, wide, octs), out_shape=jax.Shape...]
where the time goes in v3:
time: 21.2 us; the launch traced here: 21 us
  Pallas kernels  16.8 us (79%)
  local copies, waits for them, and re-layouts  4.1 us (19%)
    pallas_call x1, Pallas kernels, on_device(): pl.pallas_call(functools.partial(kernel, wide, octs), out_shape=jax.Shape...  16.8 us
    unnamed x11, local copies, waits for them, and re-layouts  4.1 us

profile of v3, /device:TPU:0, one launch (start us, length us, event | category | flops | bytes accessed | tf_op | source)
XLA Modules:
  0.0 21.0 jit_solution(17082799383092593805)
XLA Ops:
  0.0 0.0 copy-start.4
  0.0 0.7 %copy-done.4 = s32[8]{0:T(128)S(1)} copy-done((s32[8]{0:T(128)S(1)}, s32[8]{0:T(128)}, u32[]{:S(2)}) %copy-start.4) | copy-done | bytes 56
  0.7 0.0 copy-start
  0.7 0.8 %copy-done = f32[3,2048]{1,0:T(4,128)S(1)} copy-done((f32[3,2048]{1,0:T(4,128)S(1)}, f32[3,2048]{1,0:T(4,128)}, u32[]{:S(2)}) %copy-start) | copy-done | bytes 24600
  1.4 0.0 copy-start.1
  1.4 0.7 %copy-done.1 = f32[2048]{0:T(1024)S(1)} copy-done((f32[2048]{0:T(1024)S(1)}, f32[2048]{0:T(1024)}, u32[]{:S(2)}) %copy-start.1) | copy-done | bytes 8216
  2.1 0.0 copy-start.2
  2.1 0.7 %copy-done.2 = s32[8,8]{1,0:T(8,128)S(1)} copy-done((s32[8,8]{1,0:T(8,128)S(1)}, s32[8,8]{1,0:T(8,128)}, u32[]{:S(2)}) %copy-start.2) | copy-done | bytes 280
  2.8 0.0 copy-start.3
  2.8 0.7 %copy-done.3 = s32[8,16]{1,0:T(8,128)S(1)} copy-done((s32[8,16]{1,0:T(8,128)S(1)}, s32[8,16]{1,0:T(8,128)}, u32[]{:S(2)}) %copy-start.3) | copy-done | bytes 536
  3.5 16.8 %shard_map.55 = f32[3,2048]{1,0:T(4,128)S(1)} custom-call(s32[8]{0:T(128)S(1)} %copy-done.4, s32[8,8]{1,0:T(8,128)S(1)} %copy-done.2, s32[8,16]{1,0:T(8,128)S(1)} %copy-done.3, f32[3,2048]{1,0:T(4,128)S(1)} %copy-done, f32[1,2048]{1,0:T(1,128)S(1)} %bitcast.1), custom_call_target="tpu_custom_call" | custom-call | tf_op jit(solution)/shard_map/pallas_call | solution.py:232
  20.3 0.6 %copy.7 = f32[3,2048]{1,0:T(4,128)} copy(f32[3,2048]{1,0:T(4,128)S(1)} %shard_map.55) | data formatting | bytes 49152
Async XLA Ops:
  0.0 0.7 %copy-start.4 = (s32[8]{0:T(128)S(1)}, s32[8]{0:T(128)}, u32[]{:S(2)}) copy-start(s32[8]{0:T(128)} %cnt_in.1) | copy-start | bytes 100
  0.7 0.8 %copy-start = (f32[3,2048]{1,0:T(4,128)S(1)}, f32[3,2048]{1,0:T(4,128)}, u32[]{:S(2)}) copy-start(f32[3,2048]{1,0:T(4,128)} %pos_in.1) | copy-start | bytes 73732
  1.4 0.7 %copy-start.1 = (f32[2048]{0:T(1024)S(1)}, f32[2048]{0:T(1024)}, u32[]{:S(2)}) copy-start(f32[2048]{0:T(1024)} %param.6) | copy-start | bytes 24580
  2.1 0.7 %copy-start.2 = (s32[8,8]{1,0:T(8,128)S(1)}, s32[8,8]{1,0:T(8,128)}, u32[]{:S(2)}) copy-start(s32[8,8]{1,0:T(8,128)} %near_in.1) | copy-start | bytes 772
  2.8 0.7 %copy-start.3 = (s32[8,16]{1,0:T(8,128)S(1)}, s32[8,16]{1,0:T(8,128)}, u32[]{:S(2)}) copy-start(s32[8,16]{1,0:T(8,128)} %far_in.1) | copy-start | bytes 1540
